TPU v7x, 512 devices: a whole 4x8x8 slice. The times are simulated.
512 devices in a mesh: rep: 8 (over z_hi, core), row: 8 (over z_lo, x), col: 8 (over y).
Axes of the slice: x: 4, y: 8, z: 8 (z_hi: 4, z_lo: 2; z = z_hi * 2 + z_lo), core: 2. Of those that a mesh axis runs over, the one named last changes fastest.
Arguments:
- inputs: bfloat16 [8, 128, 6144], P('rep', 'col', 'row'), may hold values from -6 to 6
- w_in: bfloat16 [6144, 24576], P('row', ('rep', 'col')), may hold values from -0.078125 to 0.078125
- w_out: bfloat16 [24576, 6144], P(('rep', 'col'), 'row'), may hold values from -0.0390625 to 0.0390625
- cotangent: bfloat16 [8, 128, 6144], P('rep', 'col', 'row'), may hold values from -3072 to 3072
- counts: int32 [8], replicated, may hold values from 0 to 4, as said below
Outputs:
- block_output: bfloat16 [8, 128, 6144], P('rep', 'col', 'row')
- input_grad: bfloat16 [8, 128, 6144], P('rep', 'col', 'row')
- w_in_grad: float32 [6144, 24576], P('row', ('rep', 'col'))
- w_out_grad: float32 [24576, 6144], P(('rep', 'col'), 'row')
Inputs may be any that keep to these rules, and one draw needn't show every extreme that they name: Replica r completed its first counts[r] micro-batches; at least one replica completed all 4.
All inputs are finite; a program needn't handle non-finite values.
Results may differ from a plain program's by a relative error of at most 0.015.
Values may be sent and summed in bfloat16 or wider, within the bound.
No kernel may reach another device: no remote copies, remote signals or barrier semaphores. Data moves between devices by JAX's collectives and lax.ppermute only.
A program may use at most 64 MiB of HBM per device.

v0:
```python
import jax
import jax.numpy as jnp
from jax import lax
from jax.sharding import PartitionSpec as P

MBT = 32
root_coef = 0.7978845608028654
cubic_coef = 0.044715


def in_one_piece(arrays, axis, dim, along):
    both = jnp.concatenate(arrays, axis=along)
    result, at, finished = (lax.all_gather(both, axis, axis=dim, tiled=True), 0, [])
    for a in arrays:
        finished.append(lax.slice_in_dim(result, at, at + a.shape[along], axis=along))
        at += a.shape[along]
    return tuple(finished)


def split_up(value, dim, size):
    dims = value.shape
    pieces = value.reshape(*dims[:dim], size, dims[dim] // size, *dims[dim + 1 :])
    return jnp.moveaxis(pieces, dim, 0)


def summed_on_arrival(value, axis, dim):
    size = lax.axis_size(axis)
    pieces = lax.all_to_all(split_up(value, dim, size), axis, 0, 0, tiled=True)
    return jnp.sum(pieces.astype(jnp.float32), axis=0)


def sent_to_all(value, axis):
    size = lax.axis_size(axis)
    return lax.all_to_all(
        jnp.broadcast_to(value[None], (size, *value.shape)), axis, 0, 0, tiled=True
    )


def joined_along(pieces, dim):
    pieces = jnp.moveaxis(pieces, 0, dim)
    dims = pieces.shape
    return pieces.reshape(*dims[:dim], dims[dim] * dims[dim + 1], *dims[dim + 2 :])


def gathered_copies(value, axis, dim):
    pieces = sent_to_all(value, axis)
    return joined_along(pieces, dim)


def gelu_tanh(values):
    inner = root_coef * (values + cubic_coef * values * values * values)
    return 0.5 * values * (1.0 + jnp.tanh(inner))


def gelu_slope(values):
    inner = root_coef * (values + cubic_coef * values * values * values)
    tangent = jnp.tanh(inner)
    return 0.5 * (1.0 + tangent) + 0.5 * values * (1.0 - tangent * tangent) * root_coef * (
        1.0 + 3.0 * cubic_coef * values * values
    )


def right_product(left, right):
    return lax.dot_general(
        left, right, (((1,), (1,)), ((), ())), preferred_element_type=jnp.float32
    )


def first_product(left, right):
    return lax.dot_general(
        left, right, (((0,), (0,)), ((), ())), preferred_element_type=jnp.float32
    )


def body(inputs, w_in, w_out, cotangent, counts):
    rows_local = inputs.shape[1]
    width_local = inputs.shape[2]
    tokens_local = inputs.reshape(rows_local, width_local)
    replicas = lax.axis_size("rep")
    replica_index = lax.axis_index("rep")
    column_index = lax.axis_index("col")
    own_count = jnp.sum(jnp.where(jnp.arange(replicas) == replica_index, counts, 0))
    token_total = (MBT * jnp.sum(counts)).astype(jnp.float32)
    positions = column_index * rows_local + jnp.arange(rows_local, dtype=jnp.int32)
    kept_mask = (positions // MBT < own_count).astype(jnp.float32)
    scaled = (
        cotangent.reshape(rows_local, width_local).astype(jnp.float32)
        * kept_mask[:, None]
        / token_total
    ).astype(jnp.bfloat16)
    tokens_all, scaled_all = in_one_piece((tokens_local, scaled), "col", 0, 1)
    inner_cols = lax.all_gather(w_in, "rep", axis=1, tiled=True)
    outer_rows = lax.all_gather(w_out, "rep", axis=0, tiled=True)
    partial_hidden = jnp.dot(tokens_all, inner_cols, preferred_element_type=jnp.float32)
    hidden = summed_on_arrival(partial_hidden.astype(jnp.bfloat16), "row", 0)
    active_share = gelu_tanh(hidden).astype(jnp.bfloat16)
    activated = gathered_copies(active_share, "row", 0)
    output_terms = jnp.dot(activated, outer_rows, preferred_element_type=jnp.float32)
    output_local = summed_on_arrival(output_terms.astype(jnp.bfloat16), "col", 0)
    block_output = (tokens_local.astype(jnp.float32) + output_local).astype(jnp.bfloat16)
    slope_terms = right_product(scaled_all, outer_rows)
    slope_sum = summed_on_arrival(slope_terms.astype(jnp.bfloat16), "row", 0)
    grad_share = (slope_sum * gelu_slope(hidden)).astype(jnp.bfloat16)
    hidden_grad = gathered_copies(grad_share, "row", 0)
    back_terms = right_product(hidden_grad, inner_cols)
    back_local = summed_on_arrival(back_terms.astype(jnp.bfloat16), "col", 0)
    input_grad = (scaled.astype(jnp.float32) + back_local).astype(jnp.bfloat16)
    token_reps, scaled_reps = in_one_piece((tokens_all, scaled_all), "rep", 0, 1)
    hidden_reps, active_reps = (
        lax.all_to_all(hidden_grad, "rep", split_axis=1, concat_axis=0, tiled=True),
        lax.all_to_all(activated, "rep", split_axis=1, concat_axis=0, tiled=True),
    )
    w_in_grad = first_product(token_reps, hidden_reps)
    w_out_grad = first_product(active_reps, scaled_reps)
    return (
        block_output.reshape(1, rows_local, width_local),
        input_grad.reshape(1, rows_local, width_local),
        w_in_grad,
        w_out_grad,
    )


def solution(mesh):
    placed = (
        P("rep", "col", "row"),
        P("row", ("rep", "col")),
        P(("rep", "col"), "row"),
        P("rep", "col", "row"),
        P(),
    )
    return jax.shard_map(
        body,
        mesh=mesh,
        in_specs=placed,
        out_specs=(
            P("rep", "col", "row"),
            P("rep", "col", "row"),
            P("row", ("rep", "col")),
            P(("rep", "col"), "row"),
        ),
        check_vma=False,
    )
```

profile of v0, /device:TPU:2, one launch (start us, length us, event | category | flops | bytes accessed | tf_op | source)
XLA Modules:
  0.0 305.8 jit_solution(1008410382800476033)
XLA Ops:
  8.7 1.3 fusion.20
  11.3 0.8 fusion.15
  12.1 0.7 pad_maximum_fusion
  12.8 26.6 %all_gather.12 = bf16[128,1536]{1,0:T(8,128)(2,1)S(1)} all-gather(bf16[16,1536]{1,0:T(8,128)(2,1)S(1)} %pad_maximum_fusion), channel_id=1, replica_groups=mesh['rep'=8,'row'=8,'col'=8] {'col'}, dimensions={0}, use_global_device_ids=true | all-gather | bytes 442368 | tf_op jit(solution)/shard_map/all_gather | solution.py:13
  39.4 35.9 %all-gather.6.cloned.1.call-done = bf16[3072,768]{1,0:T(8,128)(2,1)} async-done(((bf16[384,768]{1,0:T(8,128)(2,1)}), bf16[3072,768]{1,0:T(8,128)(2,1)}) %all-gather.6.cloned.1.call-update) | async-done | bytes 4718608 | tf_op jit(solution)/shard_map/all_gather | solution.py:93
  75.3 4.9 %convolution_convert_fusion = bf16[128,3072]{1,0:T(8,128)(2,1)} fusion(bf16[3072,768]{1,0:T(8,128)(2,1)} %all-gather.6.cloned.1.call-done, bf16[128,1536]{1,0:T(8,128)(2,1)S(1)} %all_gather.12), kind=kOutput, calls=%fused_computation | convolution fusion | flops 604372992 | bytes 5701632 | tf_op jit(solution)/shard_map/dot_general | solution.py:64
  80.2 4.8 %all-to-all-start.3 = ((bf16[8,16,3072]{2,1,0:T(8,128)(2,1)}), bf16[8,16,3072]{2,1,0:T(8,128)(2,1)S(1)}, u32[]{:S(2)}, u32[]{:S(2)}) async-start(bf16[8,16,3072]{2,1,0:T(8,128)(2,1)} %bitcast.6), calls=%async_computation.3 | async-start | bytes 1572864 | tf_op jit(solution)/shard_map/all_to_all | solution.py:28
  85.0 53.2 %all-gather.4.cloned.1.call-done = bf16[768,3072]{1,0:T(8,128)(2,1)} async-done(((bf16[768,384]{1,0:T(8,128)(2,1)}), bf16[768,3072]{1,0:T(8,128)(2,1)}) %all-gather.4.cloned.1.call-update) | async-done | bytes 4718608 | tf_op jit(solution)/shard_map/all_gather | solution.py:92
  138.2 4.1 %convolution_convert_fusion.1 = bf16[128,3072]{1,0:T(8,128)(2,1)} fusion(bf16[768,3072]{1,0:T(8,128)(2,1)} %all-gather.4.cloned.1.call-done, bf16[128,1536]{1,0:T(8,128)(2,1)S(1)} %all_gather.12), kind=kOutput, calls=%fused_computation.1 | convolution fusion | flops 604372992 | bytes 5701632 | tf_op jit(solution)/shard_map/dot_general | solution.py:94
  142.3 4.8 %all-to-all-start = ((bf16[8,16,3072]{2,1,0:T(8,128)(2,1)}), bf16[8,16,3072]{2,1,0:T(8,128)(2,1)S(1)}, u32[]{:S(2)}, u32[]{:S(2)}) async-start(bf16[8,16,3072]{2,1,0:T(8,128)(2,1)} %bitcast.2), calls=%async_computation | async-start | bytes 1572864 | tf_op jit(solution)/shard_map/all_to_all | solution.py:28
  147.2 11.1 %all-to-all-done = bf16[8,16,3072]{2,1,0:T(8,128)(2,1)S(1)} async-done(((bf16[8,16,3072]{2,1,0:T(8,128)(2,1)}), bf16[8,16,3072]{2,1,0:T(8,128)(2,1)S(1)}, u32[]{:S(2)}, u32[]{:S(2)}) %all-to-all-start) | async-done | bytes 786464 | tf_op jit(solution)/shard_map/all_to_all | solution.py:28
  158.6 1.0 broadcast_in_dim.9
  159.6 4.8 %all-to-all-start.1 = ((bf16[8,16,3072]{2,1,0:T(8,128)(2,1)}), bf16[8,16,3072]{2,1,0:T(8,128)(2,1)S(1)}, u32[]{:S(2)}, u32[]{:S(2)}) async-start(bf16[8,16,3072]{2,1,0:T(8,128)(2,1)} %broadcast_in_dim.9), calls=%async_computation.1 | async-start | bytes 1572864 | tf_op jit(solution)/shard_map/all_to_all | solution.py:34
  164.4 0.7 all-gather.8.cloned.1.call-update
  165.1 10.3 %all-to-all-done.1 = bf16[8,16,3072]{2,1,0:T(8,128)(2,1)S(1)} async-done(((bf16[8,16,3072]{2,1,0:T(8,128)(2,1)}), bf16[8,16,3072]{2,1,0:T(8,128)(2,1)S(1)}, u32[]{:S(2)}, u32[]{:S(2)}) %all-to-all-start.1) | async-done | bytes 786464 | tf_op jit(solution)/shard_map/all_to_all | solution.py:34
  175.4 1.0 broadcast_in_dim.10
  176.3 4.8 %all-to-all-start.4 = ((bf16[8,16,3072]{2,1,0:T(8,128)(2,1)}), bf16[8,16,3072]{2,1,0:T(8,128)(2,1)S(1)}, u32[]{:S(2)}, u32[]{:S(2)}) async-start(bf16[8,16,3072]{2,1,0:T(8,128)(2,1)} %broadcast_in_dim.10), calls=%async_computation.4 | async-start | bytes 1572864 | tf_op jit(solution)/shard_map/all_to_all | solution.py:34
  181.2 3.8 %convolution_convert_fusion.3 = bf16[128,768]{1,0:T(8,128)(2,1)} fusion(bf16[128,3072]{1,0:T(8,128)(2,1)S(1)} %bitcast.43, bf16[3072,768]{1,0:T(8,128)(2,1)} %all-gather.6.cloned.1.call-done), kind=kOutput, calls=%fused_computation.9 | convolution fusion | flops 604078080 | bytes 5701632 | tf_op jit(solution)/shard_map/dot_general | solution.py:98
  185.0 26.9 %all-to-all-done.4 = bf16[8,16,3072]{2,1,0:T(8,128)(2,1)S(1)} async-done(((bf16[8,16,3072]{2,1,0:T(8,128)(2,1)}), bf16[8,16,3072]{2,1,0:T(8,128)(2,1)S(1)}, u32[]{:S(2)}, u32[]{:S(2)}) %all-to-all-start.4) | async-done | bytes 786464 | tf_op jit(solution)/shard_map/all_to_all | solution.py:34
  211.9 6.9 %all-to-all-start.2 = ((bf16[8,16,768]{2,1,0:T(8,128)(2,1)}), bf16[8,16,768]{2,1,0:T(8,128)(2,1)S(1)}, u32[]{:S(2)}, u32[]{:S(2)}) async-start(bf16[8,16,768]{2,1,0:T(8,128)(2,1)} %bitcast.4), calls=%async_computation.2 | async-start | bytes 393216 | tf_op jit(solution)/shard_map/all_to_all | solution.py:28
  218.8 4.7 %convolution_convert_fusion.2 = bf16[128,768]{1,0:T(8,128)(2,1)} fusion(bf16[128,3072]{1,0:T(8,128)(2,1)S(1)} %bitcast.45, bf16[768,3072]{1,0:T(8,128)(2,1)} %all-gather.4.cloned.1.call-done), kind=kOutput, calls=%fused_computation.8 | convolution fusion | flops 604078080 | bytes 5701632 | tf_op jit(solution)/shard_map/dot_general | solution.py:64
  223.5 5.3 %all-to-all-done.2 = bf16[8,16,768]{2,1,0:T(8,128)(2,1)S(1)} async-done(((bf16[8,16,768]{2,1,0:T(8,128)(2,1)}), bf16[8,16,768]{2,1,0:T(8,128)(2,1)S(1)}, u32[]{:S(2)}, u32[]{:S(2)}) %all-to-all-start.2) | async-done | bytes 196640 | tf_op jit(solution)/shard_map/all_to_all | solution.py:28
  228.7 3.4 %all-to-all-start.5 = ((bf16[8,16,768]{2,1,0:T(8,128)(2,1)}), bf16[8,16,768]{2,1,0:T(8,128)(2,1)S(1)}, u32[]{:S(2)}, u32[]{:S(2)}) async-start(bf16[8,16,768]{2,1,0:T(8,128)(2,1)} %bitcast.8), calls=%async_computation.5 | async-start | bytes 393216 | tf_op jit(solution)/shard_map/all_to_all | solution.py:28
  232.3 1.0 copy.11
  233.3 8.6 %all-to-all-done.5 = bf16[8,16,768]{2,1,0:T(8,128)(2,1)S(1)} async-done(((bf16[8,16,768]{2,1,0:T(8,128)(2,1)}), bf16[8,16,768]{2,1,0:T(8,128)(2,1)S(1)}, u32[]{:S(2)}, u32[]{:S(2)}) %all-to-all-start.5) | async-done | bytes 196640 | tf_op jit(solution)/shard_map/all_to_all | solution.py:28
  241.8 3.5 %all-to-all-start.6 = ((bf16[128,8,384]{2,0,1:T(8,128)(2,1)}), bf16[128,8,384]{2,0,1:T(8,128)(2,1)S(1)}, u32[]{:S(2)}, u32[]{:S(2)}) async-start(bf16[128,8,384]{2,0,1:T(8,128)(2,1)} %copy.11), calls=%async_computation.6 | async-start | bytes 1572864 | tf_op jit(solution)/shard_map/all_to_all | solution.py:110
  245.5 1.0 copy.12
  246.5 22.3 %all-to-all-done.6 = bf16[128,8,384]{2,0,1:T(8,128)(2,1)S(1)} async-done(((bf16[128,8,384]{2,0,1:T(8,128)(2,1)}), bf16[128,8,384]{2,0,1:T(8,128)(2,1)S(1)}, u32[]{:S(2)}, u32[]{:S(2)}) %all-to-all-start.6) | async-done | bytes 786464 | tf_op jit(solution)/shard_map/all_to_all | solution.py:110
  268.8 3.5 %all-to-all-start.7 = ((bf16[128,8,384]{2,0,1:T(8,128)(2,1)}), bf16[128,8,384]{2,0,1:T(8,128)(2,1)S(1)}, u32[]{:S(2)}, u32[]{:S(2)}) async-start(bf16[128,8,384]{2,0,1:T(8,128)(2,1)} %copy.12), calls=%async_computation.7 | async-start | bytes 1572864 | tf_op jit(solution)/shard_map/all_to_all | solution.py:111
  273.8 3.4 %fusion.2 = f32[768,384]{1,0:T(8,128)} fusion(bf16[1024,384]{1,0:T(8,128)(2,1)S(1)} %bitcast.49, bf16[1024,1536]{1,0:T(8,128)(2,1)} %all-gather.8.cloned.1.call-done), kind=kOutput, calls=%fused_computation.4 | convolution fusion | flops 603979776 | bytes 3538944 | tf_op jit(solution)/shard_map/dot_general | solution.py:70
  277.2 18.9 %all-to-all-done.7 = bf16[128,8,384]{2,0,1:T(8,128)(2,1)S(1)} async-done(((bf16[128,8,384]{2,0,1:T(8,128)(2,1)}), bf16[128,8,384]{2,0,1:T(8,128)(2,1)S(1)}, u32[]{:S(2)}, u32[]{:S(2)}) %all-to-all-start.7) | async-done | bytes 786464 | tf_op jit(solution)/shard_map/all_to_all | solution.py:111
  296.1 3.2 %fusion = f32[384,768]{1,0:T(8,128)} fusion(bf16[1024,384]{1,0:T(8,128)(2,1)S(1)} %bitcast.50, bf16[1024,1536]{1,0:T(8,128)(2,1)} %all-gather.8.cloned.1.call-done), kind=kOutput, calls=%fused_computation.2 | convolution fusion | flops 603979776 | bytes 3538944 | tf_op jit(solution)/shard_map/dot_general | solution.py:70
  (23 shorter events, 4.1 us)
Async XLA Ops:
  7.2 68.2 %all-gather.6.cloned.1.call-start = ((), (), s32[]{:S(2)}) async-start(), calls=%async_computation.9 | async-start | bytes 5308416 | tf_op jit(solution)/shard_map/all_gather | solution.py:93
  7.9 130.3 %all-gather.4.cloned.1.call-start = ((), (), s32[]{:S(2)}) async-start(), calls=%async_computation.8 | async-start | bytes 5308416 | tf_op jit(solution)/shard_map/all_gather | solution.py:92
  39.4 98.8 %copy-start = (bf16[128,1536]{1,0:T(8,128)(2,1)}, bf16[128,1536]{1,0:T(8,128)(2,1)S(1)}, u32[]{:S(2)}) copy-start(bf16[128,1536]{1,0:T(8,128)(2,1)S(1)} %all_gather.12) | copy-start | bytes 1179652
  80.2 62.1 %all-to-all-start.3 = ((bf16[8,16,3072]{2,1,0:T(8,128)(2,1)}), bf16[8,16,3072]{2,1,0:T(8,128)(2,1)S(1)}, u32[]{:S(2)}, u32[]{:S(2)}) async-start(bf16[8,16,3072]{2,1,0:T(8,128)(2,1)} %bitcast.6), calls=%async_computation.3 | async-start | bytes 1572864 | tf_op jit(solution)/shard_map/all_to_all | solution.py:28
  142.3 16.1 %all-to-all-start = ((bf16[8,16,3072]{2,1,0:T(8,128)(2,1)}), bf16[8,16,3072]{2,1,0:T(8,128)(2,1)S(1)}, u32[]{:S(2)}, u32[]{:S(2)}) async-start(bf16[8,16,3072]{2,1,0:T(8,128)(2,1)} %bitcast.2), calls=%async_computation | async-start | bytes 1572864 | tf_op jit(solution)/shard_map/all_to_all | solution.py:28
  159.6 15.8 %all-to-all-start.1 = ((bf16[8,16,3072]{2,1,0:T(8,128)(2,1)}), bf16[8,16,3072]{2,1,0:T(8,128)(2,1)S(1)}, u32[]{:S(2)}, u32[]{:S(2)}) async-start(bf16[8,16,3072]{2,1,0:T(8,128)(2,1)} %broadcast_in_dim.9), calls=%async_computation.1 | async-start | bytes 1572864 | tf_op jit(solution)/shard_map/all_to_all | solution.py:34
  164.4 109.4 %all-gather.8.cloned.1.call-start = ((), (), s32[]{:S(2)}) async-start(), calls=%async_computation.10 | async-start | bytes 3538944 | tf_op jit(solution)/shard_map/all_gather | solution.py:13
  176.3 35.5 %all-to-all-start.4 = ((bf16[8,16,3072]{2,1,0:T(8,128)(2,1)}), bf16[8,16,3072]{2,1,0:T(8,128)(2,1)S(1)}, u32[]{:S(2)}, u32[]{:S(2)}) async-start(bf16[8,16,3072]{2,1,0:T(8,128)(2,1)} %broadcast_in_dim.10), calls=%async_computation.4 | async-start | bytes 1572864 | tf_op jit(solution)/shard_map/all_to_all | solution.py:34
  211.9 16.9 %all-to-all-start.2 = ((bf16[8,16,768]{2,1,0:T(8,128)(2,1)}), bf16[8,16,768]{2,1,0:T(8,128)(2,1)S(1)}, u32[]{:S(2)}, u32[]{:S(2)}) async-start(bf16[8,16,768]{2,1,0:T(8,128)(2,1)} %bitcast.4), calls=%async_computation.2 | async-start | bytes 393216 | tf_op jit(solution)/shard_map/all_to_all | solution.py:28
  228.7 13.1 %all-to-all-start.5 = ((bf16[8,16,768]{2,1,0:T(8,128)(2,1)}), bf16[8,16,768]{2,1,0:T(8,128)(2,1)S(1)}, u32[]{:S(2)}, u32[]{:S(2)}) async-start(bf16[8,16,768]{2,1,0:T(8,128)(2,1)} %bitcast.8), calls=%async_computation.5 | async-start | bytes 393216 | tf_op jit(solution)/shard_map/all_to_all | solution.py:28
  233.3 39.2 %copy-start.2 = (bf16[1,16,768]{2,1,0:T(8,128)(2,1)S(1)}, bf16[1,16,768]{2,1,0:T(8,128)(2,1)}, u32[]{:S(2)}) copy-start(bf16[1,16,768]{2,1,0:T(8,128)(2,1)} %param.5) | copy-start | bytes 73732
  233.3 39.8 %copy-start.1 = (bf16[1,16,768]{2,1,0:T(8,128)(2,1)S(1)}, bf16[1,16,768]{2,1,0:T(8,128)(2,1)}, u32[]{:S(2)}) copy-start(bf16[1,16,768]{2,1,0:T(8,128)(2,1)} %param.8) | copy-start | bytes 73732
  241.8 27.0 %all-to-all-start.6 = ((bf16[128,8,384]{2,0,1:T(8,128)(2,1)}), bf16[128,8,384]{2,0,1:T(8,128)(2,1)S(1)}, u32[]{:S(2)}, u32[]{:S(2)}) async-start(bf16[128,8,384]{2,0,1:T(8,128)(2,1)} %copy.11), calls=%async_computation.6 | async-start | bytes 1572864 | tf_op jit(solution)/shard_map/all_to_all | solution.py:110
  268.8 27.3 %all-to-all-start.7 = ((bf16[128,8,384]{2,0,1:T(8,128)(2,1)}), bf16[128,8,384]{2,0,1:T(8,128)(2,1)S(1)}, u32[]{:S(2)}, u32[]{:S(2)}) async-start(bf16[128,8,384]{2,0,1:T(8,128)(2,1)} %copy.12), calls=%async_computation.7 | async-start | bytes 1572864 | tf_op jit(solution)/shard_map/all_to_all | solution.py:111
Sparse Core Ops, SparseCore 0:
  10.1 65.1 all-gather.5
  77.5 60.7 all-gather.3
  167.3 52.0 all-gather.7
where the time goes:
time: 307 us; the launch traced here: 306 us
  waiting for transfers between devices  195 us (64%)
  starting transfers between devices  36.7 us (12%)
  blocking collectives  26.6 us (9%)
  matrix products  24.1 us (8%)
  between operations  14.5 us (5%)
  other arithmetic  5.26 us (2%)
  local copies, waits for them, and re-layouts  4.15 us (1%)
    all_gather x1, waiting for transfers between devices, body(): inner_cols = lax.all_gather(w_in, 'rep', axis=1, tiled=True)  53.2 us
    all_to_all x2, waiting for transfers between devices, sent_to_all(): lax.all_to_all(jnp.broadcast_to(value[None], (size, *value.shape)), axis,...  37.2 us
    all_gather x1, waiting for transfers between devices, body(): outer_rows = lax.all_gather(w_out, 'rep', axis=0, tiled=True)  35.9 us
    all_gather x1, blocking collectives, in_one_piece(): lax.all_gather(both, axis, axis=dim, tiled=True)  26.6 us
    all_to_all x4, waiting for transfers between devices, summed_on_arrival(): pieces = lax.all_to_all(split_up(value, dim, size), axis, 0, 0, tiled=True)  25 us
    all_to_all x1, waiting for transfers between devices, body(): lax.all_to_all(hidden_grad, 'rep', split_axis=1, concat_axis=0, tiled=True)  22.3 us
    all_to_all x4, starting transfers between devices, summed_on_arrival(): pieces = lax.all_to_all(split_up(value, dim, size), axis, 0, 0, tiled=True)  19.9 us
    all_to_all x1, waiting for transfers between devices, body(): lax.all_to_all(activated, 'rep', split_axis=1, concat_axis=0, tiled=True)  18.9 us
  transfers between devices with their start and end apart: 11, of which 9 were waited for; matrix products, arithmetic and copies ran while one was open for 10% of the time, Pallas kernels for 0%

commit v1 on v0

--- a/solution.py
+++ b/solution.py
@@ -89,7 +89,10 @@
         / token_total
     ).astype(jnp.bfloat16)
     tokens_all, scaled_all = in_one_piece((tokens_local, scaled), "col", 0, 1)
-    inner_cols = lax.all_gather(w_in, "rep", axis=1, tiled=True)
+    count = lax.axis_size("rep")
+    parts = jnp.stack([w_in for _ in range(count)])
+    parts = lax.all_to_all(parts, "rep", split_axis=0, concat_axis=0)
+    inner_cols = jnp.concatenate(parts, axis=1)
     outer_rows = lax.all_gather(w_out, "rep", axis=0, tiled=True)
     partial_hidden = jnp.dot(tokens_all, inner_cols, preferred_element_type=jnp.float32)
     hidden = summed_on_arrival(partial_hidden.astype(jnp.bfloat16), "row", 0)

time: 307 us -> 353 us (1.15)
  waiting for transfers between devices: 195 us -> 221 us
  starting transfers between devices: 36.7 us -> 54.4 us
  local copies, waits for them, and re-layouts: 4.15 us -> 7.99 us
    all_gather x1 -> x0, waiting for transfers between devices: 53.2 us -> none  [body(): inner_cols = lax.all_gather(w_in, 'rep', axis=1, tiled=True)]
    all_gather x1, waiting for transfers between devices: 35.9 us -> 80.2 us  [body(): outer_rows = lax.all_gather(w_out, 'rep', axis=0, tiled=True)]
    all_to_all x0 -> x1, waiting for transfers between devices: none -> 32.6 us  [body(): parts = lax.all_to_all(parts, 'rep', split_axis=0, concat_axis=0)]
    all_to_all x0 -> x1, starting transfers between devices: none -> 10.4 us  [body(): parts = lax.all_to_all(parts, 'rep', split_axis=0, concat_axis=0)]
    all_to_all x4, waiting for transfers between devices: 25 us -> 31.8 us  [summed_on_arrival(): pieces = lax.all_to_all(split_up(value, dim, size), axis, 0, 0, tiled=True)]
    all_to_all x4, starting transfers between devices: 19.9 us -> 24.2 us  [summed_on_arrival(): pieces = lax.all_to_all(split_up(value, dim, size), axis, 0, 0, tiled=True)]
    all_to_all x2, waiting for transfers between devices: 37.2 us -> 33.4 us  [sent_to_all(): lax.all_to_all(jnp.broadcast_to(value[None], (size, *value.shape)), axis,...]
  transfers between devices with their start and end apart: 11 -> 11, of which waited for: 9 -> 10; matrix products, arithmetic and copies ran while one was open for 10% -> 9% of each run, Pallas kernels for 0% -> 0%
where the time goes in v1:
time: 353 us; the launch traced here: 352 us
  waiting for transfers between devices  221 us (63%)
  starting transfers between devices  54.4 us (15%)
  blocking collectives  26.6 us (8%)
  matrix products  24.4 us (7%)
  between operations  14.8 us (4%)
  local copies, waits for them, and re-layouts  7.99 us (2%)
    all_gather x1, waiting for transfers between devices, body(): outer_rows = lax.all_gather(w_out, 'rep', axis=0, tiled=True)  80.2 us
    all_to_all x2, waiting for transfers between devices, sent_to_all(): lax.all_to_all(jnp.broadcast_to(value[None], (size, *value.shape)), axis,...  33.4 us
    all_to_all x1, waiting for transfers between devices, body(): parts = lax.all_to_all(parts, 'rep', split_axis=0, concat_axis=0)  32.6 us
    all_to_all x4, waiting for transfers between devices, summed_on_arrival(): pieces = lax.all_to_all(split_up(value, dim, size), axis, 0, 0, tiled=True)  31.8 us
    all_gather x1, blocking collectives, in_one_piece(): lax.all_gather(both, axis, axis=dim, tiled=True)  26.6 us
    all_to_all x4, starting transfers between devices, summed_on_arrival(): pieces = lax.all_to_all(split_up(value, dim, size), axis, 0, 0, tiled=True)  24.2 us
    all_to_all x1, waiting for transfers between devices, body(): lax.all_to_all(hidden_grad, 'rep', split_axis=1, concat_axis=0, tiled=True)  22.9 us
    all_to_all x1, waiting for transfers between devices, body(): lax.all_to_all(activated, 'rep', split_axis=1, concat_axis=0, tiled=True)  18.5 us
  transfers between devices with their start and end apart: 11, of which 10 were waited for; matrix products, arithmetic and copies ran while one was open for 9% of the time, Pallas kernels for 0%

profile of v1, /device:TPU:2, one launch (start us, length us, event | category | flops | bytes accessed | tf_op | source)
XLA Modules:
  0.0 352.0 jit_solution(13270111245365748383)
XLA Ops:
  7.9 1.3 copy.13
  9.2 2.5 stack.2
  11.7 10.4 %all-to-all-start = ((bf16[8,768,384]{1,2,0:T(8,128)(2,1)}), bf16[8,768,384]{1,2,0:T(8,128)(2,1)}, u32[]{:S(2)}, u32[]{:S(2)}) async-start(bf16[8,768,384]{1,2,0:T(8,128)(2,1)} %stack.2), calls=%async_computation | async-start | bytes 9437184 | tf_op jit(solution)/shard_map/all_to_all | solution.py:94
  24.3 26.6 %all_gather.9 = bf16[128,1536]{1,0:T(8,128)(2,1)S(1)} all-gather(bf16[16,1536]{1,0:T(8,128)(2,1)S(1)} %pad_maximum_fusion), channel_id=1, replica_groups=mesh['rep'=8,'row'=8,'col'=8] {'col'}, dimensions={0}, use_global_device_ids=true | all-gather | bytes 442368 | tf_op jit(solution)/shard_map/all_gather | solution.py:13
  50.8 80.2 %all-gather.3.cloned.1.call-done = bf16[3072,768]{1,0:T(8,128)(2,1)} async-done(((bf16[384,768]{1,0:T(8,128)(2,1)}), bf16[3072,768]{1,0:T(8,128)(2,1)}) %all-gather.3.cloned.1.call-update) | async-done | bytes 4718608 | tf_op jit(solution)/shard_map/all_gather | solution.py:96
  131.1 4.9 %convolution_convert_fusion = bf16[128,3072]{1,0:T(8,128)(2,1)} fusion(bf16[3072,768]{1,0:T(8,128)(2,1)} %all-gather.3.cloned.1.call-done, bf16[128,1536]{1,0:T(8,128)(2,1)S(1)} %all_gather.9), kind=kOutput, calls=%fused_computation | convolution fusion | flops 604372992 | bytes 5701632 | tf_op jit(solution)/shard_map/dot_general | solution.py:64
  135.9 32.6 %all-to-all-done = bf16[8,768,384]{1,2,0:T(8,128)(2,1)} async-done(((bf16[8,768,384]{1,2,0:T(8,128)(2,1)}), bf16[8,768,384]{1,2,0:T(8,128)(2,1)}, u32[]{:S(2)}, u32[]{:S(2)}) %all-to-all-start) | async-done | bytes 4718624 | tf_op jit(solution)/shard_map/all_to_all | solution.py:94
  168.5 8.6 %all-to-all-start.4 = ((bf16[8,16,3072]{2,1,0:T(8,128)(2,1)}), bf16[8,16,3072]{2,1,0:T(8,128)(2,1)S(1)}, u32[]{:S(2)}, u32[]{:S(2)}) async-start(bf16[8,16,3072]{2,1,0:T(8,128)(2,1)} %bitcast.8), calls=%async_computation.4 | async-start | bytes 1572864 | tf_op jit(solution)/shard_map/all_to_all | solution.py:28
  177.0 4.8 %convolution_convert_fusion.1 = bf16[128,3072]{1,0:T(8,128)(2,1)} fusion(bf16[768,3072]{0,1:T(8,128)(2,1)} %bitcast.3, bf16[128,1536]{1,0:T(8,128)(2,1)S(1)} %all_gather.9), kind=kOutput, calls=%fused_computation.1 | convolution fusion | flops 604372992 | bytes 5701632 | tf_op jit(solution)/shard_map/dot_general | solution.py:97
  181.9 6.4 %all-to-all-done.4 = bf16[8,16,3072]{2,1,0:T(8,128)(2,1)S(1)} async-done(((bf16[8,16,3072]{2,1,0:T(8,128)(2,1)}), bf16[8,16,3072]{2,1,0:T(8,128)(2,1)S(1)}, u32[]{:S(2)}, u32[]{:S(2)}) %all-to-all-start.4) | async-done | bytes 786464 | tf_op jit(solution)/shard_map/all_to_all | solution.py:28
  188.3 4.8 %all-to-all-start.1 = ((bf16[8,16,3072]{2,1,0:T(8,128)(2,1)}), bf16[8,16,3072]{2,1,0:T(8,128)(2,1)S(1)}, u32[]{:S(2)}, u32[]{:S(2)}) async-start(bf16[8,16,3072]{2,1,0:T(8,128)(2,1)} %bitcast.4), calls=%async_computation.1 | async-start | bytes 1572864 | tf_op jit(solution)/shard_map/all_to_all | solution.py:28
  193.2 10.9 %all-to-all-done.1 = bf16[8,16,3072]{2,1,0:T(8,128)(2,1)S(1)} async-done(((bf16[8,16,3072]{2,1,0:T(8,128)(2,1)}), bf16[8,16,3072]{2,1,0:T(8,128)(2,1)S(1)}, u32[]{:S(2)}, u32[]{:S(2)}) %all-to-all-start.1) | async-done | bytes 786464 | tf_op jit(solution)/shard_map/all_to_all | solution.py:28
  204.3 1.0 broadcast_in_dim.9
  205.3 4.8 %all-to-all-start.2 = ((bf16[8,16,3072]{2,1,0:T(8,128)(2,1)}), bf16[8,16,3072]{2,1,0:T(8,128)(2,1)S(1)}, u32[]{:S(2)}, u32[]{:S(2)}) async-start(bf16[8,16,3072]{2,1,0:T(8,128)(2,1)} %broadcast_in_dim.9), calls=%async_computation.2 | async-start | bytes 1572864 | tf_op jit(solution)/shard_map/all_to_all | solution.py:34
  210.8 10.3 %all-to-all-done.2 = bf16[8,16,3072]{2,1,0:T(8,128)(2,1)S(1)} async-done(((bf16[8,16,3072]{2,1,0:T(8,128)(2,1)}), bf16[8,16,3072]{2,1,0:T(8,128)(2,1)S(1)}, u32[]{:S(2)}, u32[]{:S(2)}) %all-to-all-start.2) | async-done | bytes 786464 | tf_op jit(solution)/shard_map/all_to_all | solution.py:34
  221.1 1.0 broadcast_in_dim.10
  222.1 4.8 %all-to-all-start.5 = ((bf16[8,16,3072]{2,1,0:T(8,128)(2,1)}), bf16[8,16,3072]{2,1,0:T(8,128)(2,1)S(1)}, u32[]{:S(2)}, u32[]{:S(2)}) async-start(bf16[8,16,3072]{2,1,0:T(8,128)(2,1)} %broadcast_in_dim.10), calls=%async_computation.5 | async-start | bytes 1572864 | tf_op jit(solution)/shard_map/all_to_all | solution.py:34
  226.9 4.2 %convolution_convert_fusion.3 = bf16[128,768]{1,0:T(8,128)(2,1)} fusion(bf16[128,3072]{1,0:T(8,128)(2,1)S(1)} %bitcast.46, bf16[3072,768]{1,0:T(8,128)(2,1)} %all-gather.3.cloned.1.call-done), kind=kOutput, calls=%fused_computation.9 | convolution fusion | flops 604078080 | bytes 5701632 | tf_op jit(solution)/shard_map/dot_general | solution.py:101
  231.1 23.2 %all-to-all-done.5 = bf16[8,16,3072]{2,1,0:T(8,128)(2,1)S(1)} async-done(((bf16[8,16,3072]{2,1,0:T(8,128)(2,1)}), bf16[8,16,3072]{2,1,0:T(8,128)(2,1)S(1)}, u32[]{:S(2)}, u32[]{:S(2)}) %all-to-all-start.5) | async-done | bytes 786464 | tf_op jit(solution)/shard_map/all_to_all | solution.py:34
  254.2 7.4 %all-to-all-start.3 = ((bf16[8,16,768]{2,1,0:T(8,128)(2,1)}), bf16[8,16,768]{2,1,0:T(8,128)(2,1)S(1)}, u32[]{:S(2)}, u32[]{:S(2)}) async-start(bf16[8,16,768]{2,1,0:T(8,128)(2,1)} %bitcast.6), calls=%async_computation.3 | async-start | bytes 393216 | tf_op jit(solution)/shard_map/all_to_all | solution.py:28
  261.7 3.9 %convolution_convert_fusion.2 = bf16[128,768]{1,0:T(8,128)(2,1)} fusion(bf16[128,3072]{1,0:T(8,128)(2,1)S(1)} %bitcast.48, bf16[768,3072]{0,1:T(8,128)(2,1)} %bitcast.3), kind=kOutput, calls=%fused_computation.8 | convolution fusion | flops 604078080 | bytes 5701632 | tf_op jit(solution)/shard_map/dot_general | solution.py:64
  265.5 5.9 %all-to-all-done.3 = bf16[8,16,768]{2,1,0:T(8,128)(2,1)S(1)} async-done(((bf16[8,16,768]{2,1,0:T(8,128)(2,1)}), bf16[8,16,768]{2,1,0:T(8,128)(2,1)S(1)}, u32[]{:S(2)}, u32[]{:S(2)}) %all-to-all-start.3) | async-done | bytes 196640 | tf_op jit(solution)/shard_map/all_to_all | solution.py:28
  271.5 3.4 all-to-all-start.6
  275.0 1.0 copy.14
  276.0 8.6 %all-to-all-done.6 = bf16[8,16,768]{2,1,0:T(8,128)(2,1)S(1)} async-done(((bf16[8,16,768]{2,1,0:T(8,128)(2,1)}), bf16[8,16,768]{2,1,0:T(8,128)(2,1)S(1)}, u32[]{:S(2)}, u32[]{:S(2)}) %all-to-all-start.6) | async-done | bytes 196640 | tf_op jit(solution)/shard_map/all_to_all | solution.py:28
  284.5 6.5 %all-to-all-start.7 = ((bf16[128,8,384]{2,0,1:T(8,128)(2,1)}), bf16[128,8,384]{2,0,1:T(8,128)(2,1)S(1)}, u32[]{:S(2)}, u32[]{:S(2)}) async-start(bf16[128,8,384]{2,0,1:T(8,128)(2,1)} %copy.14), calls=%async_computation.7 | async-start | bytes 1572864 | tf_op jit(solution)/shard_map/all_to_all | solution.py:113
  291.2 1.0 copy.15
  292.2 22.9 %all-to-all-done.7 = bf16[128,8,384]{2,0,1:T(8,128)(2,1)S(1)} async-done(((bf16[128,8,384]{2,0,1:T(8,128)(2,1)}), bf16[128,8,384]{2,0,1:T(8,128)(2,1)S(1)}, u32[]{:S(2)}, u32[]{:S(2)}) %all-to-all-start.7) | async-done | bytes 786464 | tf_op jit(solution)/shard_map/all_to_all | solution.py:113
  315.1 3.5 %all-to-all-start.8 = ((bf16[128,8,384]{2,0,1:T(8,128)(2,1)}), bf16[128,8,384]{2,0,1:T(8,128)(2,1)S(1)}, u32[]{:S(2)}, u32[]{:S(2)}) async-start(bf16[128,8,384]{2,0,1:T(8,128)(2,1)} %copy.15), calls=%async_computation.8 | async-start | bytes 1572864 | tf_op jit(solution)/shard_map/all_to_all | solution.py:114
  320.0 3.4 fusion.2
  323.4 18.5 %all-to-all-done.8 = bf16[128,8,384]{2,0,1:T(8,128)(2,1)S(1)} async-done(((bf16[128,8,384]{2,0,1:T(8,128)(2,1)}), bf16[128,8,384]{2,0,1:T(8,128)(2,1)S(1)}, u32[]{:S(2)}, u32[]{:S(2)}) %all-to-all-start.8) | async-done | bytes 786464 | tf_op jit(solution)/shard_map/all_to_all | solution.py:114
  341.9 3.2 fusion
  (26 shorter events, 4.8 us)
Async XLA Ops:
  7.2 123.9 %all-gather.3.cloned.1.call-start = ((), (), s32[]{:S(2)}) async-start(), calls=%async_computation.9 | async-start | bytes 5308416 | tf_op jit(solution)/shard_map/all_gather | solution.py:96
  11.7 10.4 %copy-start.3 = (s32[8]{0:T(128)S(1)}, s32[8]{0:T(128)}, u32[]{:S(2)}) copy-start(s32[8]{0:T(128)} %param.9) | copy-start | bytes 100
  11.7 12.4 %copy-start.1 = (bf16[1,16,768]{2,1,0:T(8,128)(2,1)S(1)}, bf16[1,16,768]{2,1,0:T(8,128)(2,1)}, u32[]{:S(2)}) copy-start(bf16[1,16,768]{2,1,0:T(8,128)(2,1)} %param.8) | copy-start | bytes 73732
  11.7 12.5 %copy-start.2 = (bf16[1,16,768]{2,1,0:T(8,128)(2,1)S(1)}, bf16[1,16,768]{2,1,0:T(8,128)(2,1)}, u32[]{:S(2)}) copy-start(bf16[1,16,768]{2,1,0:T(8,128)(2,1)} %param.5) | copy-start | bytes 73732
  11.7 156.7 %all-to-all-start = ((bf16[8,768,384]{1,2,0:T(8,128)(2,1)}), bf16[8,768,384]{1,2,0:T(8,128)(2,1)}, u32[]{:S(2)}, u32[]{:S(2)}) async-start(bf16[8,768,384]{1,2,0:T(8,128)(2,1)} %stack.2), calls=%async_computation | async-start | bytes 9437184 | tf_op jit(solution)/shard_map/all_to_all | solution.py:94
  50.8 126.2 %copy-start = (bf16[128,1536]{1,0:T(8,128)(2,1)}, bf16[128,1536]{1,0:T(8,128)(2,1)S(1)}, u32[]{:S(2)}) copy-start(bf16[128,1536]{1,0:T(8,128)(2,1)S(1)} %all_gather.9) | copy-start | bytes 1179652
  168.5 19.8 %all-to-all-start.4 = ((bf16[8,16,3072]{2,1,0:T(8,128)(2,1)}), bf16[8,16,3072]{2,1,0:T(8,128)(2,1)S(1)}, u32[]{:S(2)}, u32[]{:S(2)}) async-start(bf16[8,16,3072]{2,1,0:T(8,128)(2,1)} %bitcast.8), calls=%async_computation.4 | async-start | bytes 1572864 | tf_op jit(solution)/shard_map/all_to_all | solution.py:28
  188.3 15.8 %all-to-all-start.1 = ((bf16[8,16,3072]{2,1,0:T(8,128)(2,1)}), bf16[8,16,3072]{2,1,0:T(8,128)(2,1)S(1)}, u32[]{:S(2)}, u32[]{:S(2)}) async-start(bf16[8,16,3072]{2,1,0:T(8,128)(2,1)} %bitcast.4), calls=%async_computation.1 | async-start | bytes 1572864 | tf_op jit(solution)/shard_map/all_to_all | solution.py:28
  205.3 15.8 %all-to-all-start.2 = ((bf16[8,16,3072]{2,1,0:T(8,128)(2,1)}), bf16[8,16,3072]{2,1,0:T(8,128)(2,1)S(1)}, u32[]{:S(2)}, u32[]{:S(2)}) async-start(bf16[8,16,3072]{2,1,0:T(8,128)(2,1)} %broadcast_in_dim.9), calls=%async_computation.2 | async-start | bytes 1572864 | tf_op jit(solution)/shard_map/all_to_all | solution.py:34
  210.1 109.9 %all-gather.5.cloned.1.call-start = ((), (), s32[]{:S(2)}) async-start(), calls=%async_computation.10 | async-start | bytes 3538944 | tf_op jit(solution)/shard_map/all_gather | solution.py:13
  222.1 32.2 %all-to-all-start.5 = ((bf16[8,16,3072]{2,1,0:T(8,128)(2,1)}), bf16[8,16,3072]{2,1,0:T(8,128)(2,1)S(1)}, u32[]{:S(2)}, u32[]{:S(2)}) async-start(bf16[8,16,3072]{2,1,0:T(8,128)(2,1)} %broadcast_in_dim.10), calls=%async_computation.5 | async-start | bytes 1572864 | tf_op jit(solution)/shard_map/all_to_all | solution.py:34
  254.2 17.2 %all-to-all-start.3 = ((bf16[8,16,768]{2,1,0:T(8,128)(2,1)}), bf16[8,16,768]{2,1,0:T(8,128)(2,1)S(1)}, u32[]{:S(2)}, u32[]{:S(2)}) async-start(bf16[8,16,768]{2,1,0:T(8,128)(2,1)} %bitcast.6), calls=%async_computation.3 | async-start | bytes 393216 | tf_op jit(solution)/shard_map/all_to_all | solution.py:28
  271.5 13.1 %all-to-all-start.6 = ((bf16[8,16,768]{2,1,0:T(8,128)(2,1)}), bf16[8,16,768]{2,1,0:T(8,128)(2,1)S(1)}, u32[]{:S(2)}, u32[]{:S(2)}) async-start(bf16[8,16,768]{2,1,0:T(8,128)(2,1)} %bitcast.11), calls=%async_computation.6 | async-start | bytes 393216 | tf_op jit(solution)/shard_map/all_to_all | solution.py:28
  284.5 30.5 %all-to-all-start.7 = ((bf16[128,8,384]{2,0,1:T(8,128)(2,1)}), bf16[128,8,384]{2,0,1:T(8,128)(2,1)S(1)}, u32[]{:S(2)}, u32[]{:S(2)}) async-start(bf16[128,8,384]{2,0,1:T(8,128)(2,1)} %copy.14), calls=%async_computation.7 | async-start | bytes 1572864 | tf_op jit(solution)/shard_map/all_to_all | solution.py:113
  315.1 26.8 %all-to-all-start.8 = ((bf16[128,8,384]{2,0,1:T(8,128)(2,1)}), bf16[128,8,384]{2,0,1:T(8,128)(2,1)S(1)}, u32[]{:S(2)}, u32[]{:S(2)}) async-start(bf16[128,8,384]{2,0,1:T(8,128)(2,1)} %copy.15), calls=%async_computation.8 | async-start | bytes 1572864 | tf_op jit(solution)/shard_map/all_to_all | solution.py:114
Sparse Core Ops, SparseCore 0:
  10.1 120.8 all-gather.2
  213.0 51.8 all-gather.4
